TPU v7x, 256 devices: a whole 4x4x8 slice. The times are simulated.
256 devices in a mesh: img: 32 (over z, x), txt: 8 (over y, core).
Axes of the slice: x: 4, y: 4, z: 8, core: 2. Of those that a mesh axis runs over, the one named last changes fastest.
Arguments:
- image_pooled: bfloat16 [16384, 1664], P('img', 'txt'), may hold values from -6 to 6
- text_pooled: bfloat16 [16384, 1280], P('txt', 'img'), may hold values from -6 to 6
- image_proj: bfloat16 [1664, 1280], P('txt'), may hold values from -1.5 to 1.5
- text_proj: bfloat16 [1280, 1280], P('img'), may hold values from -2 to 2
- teacher_scale: float32 [1], replicated, may hold values from 280 to 400
Outputs:
- image_targets: float32 [16384, 16384], P('img', 'txt')
- text_targets: float32 [16384, 16384], P('img', 'txt')
All inputs are finite; a program needn't handle non-finite values.
Results may differ from a plain program's by a relative error of at most 0.0011.
Values may be sent and summed in bfloat16 or wider, within the bound.
No kernel may reach another device: no remote copies, remote signals or barrier semaphores. Data moves between devices by JAX's collectives and lax.ppermute only.
A program may use at most 64 MiB of HBM per device.

v0:
```python
import math
import jax
import jax.numpy as jnp
from jax import lax
from jax.sharding import PartitionSpec as P


def unit_rows(values):
    scale_rows = lax.rsqrt(jnp.mean(values * values, axis=-1, keepdims=True) + 1e-06)
    return (values * scale_rows / math.sqrt(values.shape[-1])).astype(jnp.bfloat16)


def add_rows(left_side, portion):
    return jnp.dot(left_side, portion, preferred_element_type=jnp.float32)


def on_device(image_pooled, text_pooled, image_proj, text_proj, teacher_scale):
    image_full = lax.all_gather(image_pooled, "txt", axis=1, tiled=True)
    image_sum = add_rows(image_full, lax.all_gather(image_proj, "txt", axis=0, tiled=True))
    image_unit = unit_rows(image_sum)
    weight_full = lax.all_gather(text_proj, "img", axis=0, tiled=True)
    text_full = lax.all_gather(text_pooled, "img", axis=1, tiled=True)
    text_unit = unit_rows(jnp.dot(text_full, weight_full, preferred_element_type=jnp.float32))
    similar = lax.dot_general(
        image_unit, text_unit, (((1,), (1,)), ((), ())), preferred_element_type=jnp.float32
    )
    logits = teacher_scale[0] * similar
    row_top = jnp.max(logits, axis=1, keepdims=True)
    col_top = jnp.max(logits, axis=0, keepdims=True)
    row_top = lax.pmax(row_top, "txt")
    col_top = lax.pmax(col_top, "img")
    row_total = lax.psum(jnp.sum(jnp.exp(logits - row_top), axis=1, keepdims=True), "txt")
    col_total = lax.psum(jnp.sum(jnp.exp(logits - col_top), axis=0, keepdims=True), "img")
    image_targets = logits - (row_top + jnp.log(row_total))
    text_targets = logits - (col_top + jnp.log(col_total))
    return (image_targets, text_targets)


def solution(mesh):
    placed = (P("img", "txt"), P("txt", "img"), P("txt", None), P("img", None), P())
    return jax.shard_map(
        on_device,
        mesh=mesh,
        in_specs=placed,
        out_specs=(P("img", "txt"), P("img", "txt")),
        check_vma=False,
    )
```

profile of v0, /device:TPU:2, one launch (start us, length us, event | category | flops | bytes accessed | tf_op | source)
XLA Modules:
  0.0 444.3 jit_solution(12399462446347487872)
XLA Ops:
  7.2 0.0 all-gather.5.cloned.1.call-start
  7.2 0.7 all-gather.5.cloned.1.call-update
  7.9 0.0 all-gather.7.cloned.1.call-start
  7.9 0.7 all-gather.7.cloned.1.call-update
  8.6 0.0 all-gather.11.cloned.1.call-start
  8.7 0.7 all-gather.11.cloned.1.call-update
  9.4 0.0 all-gather.9.cloned.1.call-start
  9.4 0.5 all-gather.9.cloned.1.call-update
  10.6 29.3 %all-gather.5.cloned.1.call-done = bf16[512,1664]{0,1:T(8,128)(2,1)} async-done(((bf16[512,208]{0,1:T(8,128)(2,1)}), bf16[512,1664]{0,1:T(8,128)(2,1)}) %all-gather.5.cloned.1.call-update) | async-done | bytes 1703952 | tf_op jit(solution)/shard_map/all_gather | solution.py:18
  39.9 37.1 %all-gather.7.cloned.1.call-done = bf16[1664,1280]{1,0:T(8,128)(2,1)} async-done(((bf16[208,1280]{1,0:T(8,128)(2,1)}), bf16[1664,1280]{1,0:T(8,128)(2,1)}) %all-gather.7.cloned.1.call-update) | async-done | bytes 4259856 | tf_op jit(solution)/shard_map/all_gather | solution.py:19
  77.0 5.5 %multiply_reduce_fusion.1 = (f32[512]{0:T(512)S(1)}, f32[512,1280]{1,0:T(8,128)S(1)}) fusion(bf16[512,1664]{0,1:T(8,128)(2,1)} %all-gather.5.cloned.1.call-done, bf16[1664,1280]{1,0:T(8,128)(2,1)} %all-gather.7.cloned.1.call-done), kind=kOutput, calls=%fused_computation.9 | convolution fusion | flops 2182348288 | bytes 8587264 | tf_op jit(solution)/shard_map/dot_general | solution.py:14
  82.5 76.1 %all-gather.11.cloned.1.call-done = bf16[1280,1280]{1,0:T(8,128)(2,1)} async-done(((bf16[40,1280]{1,0:T(8,128)(2,1)}), bf16[1280,1280]{1,0:T(8,128)(2,1)}) %all-gather.11.cloned.1.call-update) | async-done | bytes 3276816 | tf_op jit(solution)/shard_map/all_gather | solution.py:21
  158.6 84.0 %all-gather.9.cloned.1.call-done = bf16[2048,1280]{0,1:T(8,128)(2,1)} async-done(((bf16[2048,40]{0,1:T(8,128)(2,1)}), bf16[2048,1280]{0,1:T(8,128)(2,1)}) %all-gather.9.cloned.1.call-update) | async-done | bytes 5242896 | tf_op jit(solution)/shard_map/all_gather | solution.py:22
  242.7 10.4 %multiply_reduce_fusion = (f32[2048]{0:T(1024)S(1)}, f32[2048,1280]{0,1:T(8,128)S(1)}) fusion(bf16[2048,1280]{0,1:T(8,128)(2,1)} %all-gather.9.cloned.1.call-done, bf16[1280,1280]{1,0:T(8,128)(2,1)} %all-gather.11.cloned.1.call-done), kind=kOutput, calls=%fused_computation.1 | convolution fusion | flops 6716127232 | bytes 19013632 | tf_op jit(solution)/shard_map/dot_general | solution.py:23
  253.1 4.7 %fusion.7 = (f32[2048]{0:T(1024)S(1)}, f32[512]{0:T(512)S(1)}, f32[512,2048]{1,0:T(8,128)}) fusion(f32[2048,1280]{0,1:T(8,128)S(1)} %get-tuple-element.9, f32[2048]{0:T(1024)S(1)} %add_rsqrt_fusion, f32[512,1280]{1,0:T(8,128)S(1)} %get-tuple-element.11, f32[512]{0:T(512)S(1)} %add_rsqrt_fusion.1, f32[]{:T(128)} %bitcast.13), kind=kOutput, calls=%fused_computation.19 | convolution fusion | flops 2697328128 | bytes 17321988 | tf_op jit(solution)/shard_map/dot_general | solution.py:24
  257.8 72.6 %pmax.15 = f32[1,2048]{1,0:T(1,128)S(1)} all-reduce(f32[1,2048]{1,0:T(1,128)S(1)} %bitcast.20), channel_id=1, replica_groups=mesh['img'=32,'txt'=8] {'img'}, use_global_device_ids=true, to_apply=%region_7.0 | all-reduce | flops 2048 | bytes 16384 | tf_op jit(solution)/shard_map/pmax | solution.py:31
  330.4 12.4 %pmax.14 = f32[512,1]{0,1:T(1,128)S(1)} all-reduce(f32[512,1]{0,1:T(1,128)S(1)} %bitcast.21), channel_id=1, replica_groups=mesh['img'=32,'txt'=8] {'txt'}, use_global_device_ids=true, to_apply=%region_3.0 | all-reduce | flops 512 | bytes 4096 | tf_op jit(solution)/shard_map/pmax | solution.py:30
  342.8 3.4 exponential_reduce_fusion
  346.2 12.4 %psum.14 = f32[512,1]{0,1:T(1,128)S(1)} all-reduce(f32[512,1]{0,1:T(1,128)S(1)} %bitcast.18), channel_id=1, replica_groups=mesh['img'=32,'txt'=8] {'txt'}, use_global_device_ids=true, to_apply=%region_5.0 | all-reduce | flops 512 | bytes 4096 | tf_op jit(solution)/shard_map/psum | solution.py:32
  358.7 73.0 %psum.15 = f32[1,2048]{1,0:T(1,128)S(1)} all-reduce(f32[1,2048]{1,0:T(1,128)S(1)} %bitcast.16), channel_id=1, replica_groups=mesh['img'=32,'txt'=8] {'img'}, use_global_device_ids=true, to_apply=%region_9.0 | all-reduce | flops 2048 | bytes 16384 | tf_op jit(solution)/shard_map/psum | solution.py:33
  431.7 6.1 %broadcast_subtract_fusion = (f32[512,2048]{1,0:T(8,128)}, f32[512,2048]{1,0:T(8,128)}) fusion(f32[512,2048]{1,0:T(8,128)} %get-tuple-element.12, f32[2048]{0:T(1024)S(1)} %bitcast.15, f32[512]{0:T(512)S(1)} %bitcast.19), kind=kLoop, calls=%fused_computation.10 | loop fusion | flops 2097152 | bytes 12593152 | tf_op jit(solution)/shard_map/sub | solution.py:35
  (4 shorter events, 0.0 us)
Async XLA Ops:
  7.2 32.8 %all-gather.5.cloned.1.call-start = ((), (), s32[]{:S(2)}) async-start(), calls=%async_computation | async-start | bytes 1916928 | tf_op jit(solution)/shard_map/all_gather | solution.py:18
  7.9 69.1 %all-gather.7.cloned.1.call-start = ((), (), s32[]{:S(2)}) async-start(), calls=%async_computation.1 | async-start | bytes 4792320 | tf_op jit(solution)/shard_map/all_gather | solution.py:19
  8.6 150.0 %all-gather.11.cloned.1.call-start = ((), (), s32[]{:S(2)}) async-start(), calls=%async_computation.3 | async-start | bytes 3379200 | tf_op jit(solution)/shard_map/all_gather | solution.py:21
  9.4 233.3 %all-gather.9.cloned.1.call-start = ((), (), s32[]{:S(2)}) async-start(), calls=%async_computation.2 | async-start | bytes 5406720 | tf_op jit(solution)/shard_map/all_gather | solution.py:22
Sparse Core Ops, SparseCore 0:
  9.8 30.0 all-gather.4
  41.7 35.2 all-gather.6
  79.6 78.9 all-gather.10
  161.0 81.5 all-gather.8
where the time goes:
time: 445 us; the launch traced here: 444 us
  waiting for transfers between devices  229 us (51%)
  blocking collectives  170 us (38%)
  matrix products  20.6 us (5%)
  between operations  14.4 us (3%)
  other arithmetic  9.6 us (2%)
    all_gather x1, waiting for transfers between devices, on_device(): text_full = lax.all_gather(text_pooled, 'img', axis=1, tiled=True)  84 us
    all_gather x1, waiting for transfers between devices, on_device(): weight_full = lax.all_gather(text_proj, 'img', axis=0, tiled=True)  76.1 us
    psum x1, blocking collectives, on_device(): lax.psum(jnp.sum(jnp.exp(logits - col_top), axis=0, keepdims=True), 'img')  73 us
    pmax x1, blocking collectives, on_device(): col_top = lax.pmax(col_top, 'img')  72.6 us
    all_gather x1, waiting for transfers between devices, on_device(): lax.all_gather(image_proj, 'txt', axis=0, tiled=True)  37.1 us
    all_gather x1, waiting for transfers between devices, on_device(): image_full = lax.all_gather(image_pooled, 'txt', axis=1, tiled=True)  29.3 us
    pmax x1, blocking collectives, on_device(): row_top = lax.pmax(row_top, 'txt')  12.4 us
    psum x1, blocking collectives, on_device(): lax.psum(jnp.sum(jnp.exp(logits - row_top), axis=1, keepdims=True), 'txt')  12.4 us
  transfers between devices with their start and end apart: 4, of which 4 were waited for; matrix products, arithmetic and copies ran while one was open for 1% of the time, Pallas kernels for 0%

commit v1 on v0

--- a/solution.py
+++ b/solution.py
@@ -15,7 +15,9 @@
 
 
 def on_device(image_pooled, text_pooled, image_proj, text_proj, teacher_scale):
-    image_full = lax.all_gather(image_pooled, "txt", axis=1, tiled=True)
+    image_full = jnp.concatenate(
+        lax.all_to_all(jnp.stack([image_pooled] * lax.axis_size("txt")), "txt", 0, 0), axis=1
+    )
     image_sum = add_rows(image_full, lax.all_gather(image_proj, "txt", axis=0, tiled=True))
     image_unit = unit_rows(image_sum)
     weight_full = lax.all_gather(text_proj, "img", axis=0, tiled=True)

time: 445 us -> 427 us (0.960)
  waiting for transfers between devices: 229 us -> 204 us
    all_to_all x0 -> x1, waiting for transfers between devices: none -> 32.5 us  [on_device(): lax.all_to_all(jnp.stack([image_pooled] * lax.axis_size('txt')), 'txt', 0...]
    all_gather x1 -> x0, waiting for transfers between devices: 29.3 us -> none  [on_device(): image_full = lax.all_gather(image_pooled, 'txt', axis=1, tiled=True)]
    all_gather x1, waiting for transfers between devices: 37.1 us -> 8.31 us  [on_device(): lax.all_gather(image_proj, 'txt', axis=0, tiled=True)]
    all_to_all x0 -> x1, starting transfers between devices: none -> 4.47 us  [on_device(): lax.all_to_all(jnp.stack([image_pooled] * lax.axis_size('txt')), 'txt', 0...]
  transfers between devices with their start and end apart: 4 -> 4, of which waited for: 4 -> 4; matrix products, arithmetic and copies ran while one was open for 1% -> 2% of each run, Pallas kernels for 0% -> 0%
where the time goes in v1:
time: 427 us; the launch traced here: 426 us
  waiting for transfers between devices  204 us (48%)
  blocking collectives  170 us (40%)
  matrix products  21.4 us (5%)
  between operations  14.4 us (3%)
  other arithmetic  9.6 us (2%)
  starting transfers between devices  4.58 us (1%)
    all_gather x1, waiting for transfers between devices, on_device(): text_full = lax.all_gather(text_pooled, 'img', axis=1, tiled=True)  84.2 us
    all_gather x1, waiting for transfers between devices, on_device(): weight_full = lax.all_gather(text_proj, 'img', axis=0, tiled=True)  76.5 us
    psum x1, blocking collectives, on_device(): lax.psum(jnp.sum(jnp.exp(logits - col_top), axis=0, keepdims=True), 'img')  72.9 us
    pmax x1, blocking collectives, on_device(): col_top = lax.pmax(col_top, 'img')  72.6 us
    all_to_all x1, waiting for transfers between devices, on_device(): lax.all_to_all(jnp.stack([image_pooled] * lax.axis_size('txt')), 'txt', 0...  32.5 us
    pmax x1, blocking collectives, on_device(): row_top = lax.pmax(row_top, 'txt')  12.4 us
    psum x1, blocking collectives, on_device(): lax.psum(jnp.sum(jnp.exp(logits - row_top), axis=1, keepdims=True), 'txt')  12.4 us
    dot_general x1, matrix products, on_device(): jnp.dot(text_full, weight_full, preferred_element_type=jnp.float32)  10.4 us
  transfers between devices with their start and end apart: 4, of which 4 were waited for; matrix products, arithmetic and copies ran while one was open for 2% of the time, Pallas kernels for 0%

profile of v1, /device:TPU:2, one launch (start us, length us, event | category | flops | bytes accessed | tf_op | source)
XLA Modules:
  0.0 426.2 jit_solution(10597450835491962)
XLA Ops:
  7.2 0.0 all-gather.4.cloned.1.call-start
  7.2 0.7 all-gather.4.cloned.1.call-update
  7.9 0.0 all-gather.8.cloned.1.call-start
  7.9 0.7 all-gather.8.cloned.1.call-update
  8.6 0.0 all-gather.6.cloned.1.call-start
  8.7 0.7 all-gather.6.cloned.1.call-update
  9.4 2.3 stack.2
  11.6 4.5 %all-to-all-start = ((bf16[8,512,208]{1,2,0:T(8,128)(2,1)}), bf16[8,512,208]{1,2,0:T(8,128)(2,1)S(1)}, u32[]{:S(2)}, u32[]{:S(2)}) async-start(bf16[8,512,208]{1,2,0:T(8,128)(2,1)} %stack.2), calls=%async_computation | async-start | bytes 3407872 | tf_op jit(solution)/shard_map/all_to_all | solution.py:19
  16.8 32.5 %all-to-all-done = bf16[8,512,208]{1,2,0:T(8,128)(2,1)S(1)} async-done(((bf16[8,512,208]{1,2,0:T(8,128)(2,1)}), bf16[8,512,208]{1,2,0:T(8,128)(2,1)S(1)}, u32[]{:S(2)}, u32[]{:S(2)}) %all-to-all-start) | async-done | bytes 1703968 | tf_op jit(solution)/shard_map/all_to_all | solution.py:19
  49.3 8.3 %all-gather.4.cloned.1.call-done = bf16[1664,1280]{1,0:T(8,128)(2,1)} async-done(((bf16[208,1280]{1,0:T(8,128)(2,1)}), bf16[1664,1280]{1,0:T(8,128)(2,1)}) %all-gather.4.cloned.1.call-update) | async-done | bytes 4259856 | tf_op jit(solution)/shard_map/all_gather | solution.py:21
  57.6 6.3 %multiply_reduce_fusion.1 = (f32[512]{0:T(512)S(1)}, f32[512,1280]{1,0:T(8,128)}) fusion(bf16[512,1664]{0,1:T(8,128)(2,1)S(1)} %bitcast.17, bf16[1664,1280]{1,0:T(8,128)(2,1)} %all-gather.4.cloned.1.call-done), kind=kOutput, calls=%fused_computation.9 | convolution fusion | flops 2182348288 | bytes 8587264 | tf_op jit(solution)/shard_map/dot_general | solution.py:14
  63.9 0.0 copy-start
  63.9 76.5 %all-gather.8.cloned.1.call-done = bf16[1280,1280]{1,0:T(8,128)(2,1)} async-done(((bf16[40,1280]{1,0:T(8,128)(2,1)}), bf16[1280,1280]{1,0:T(8,128)(2,1)}) %all-gather.8.cloned.1.call-update) | async-done | bytes 3276816 | tf_op jit(solution)/shard_map/all_gather | solution.py:23
  140.4 84.2 %all-gather.6.cloned.1.call-done = bf16[2048,1280]{0,1:T(8,128)(2,1)} async-done(((bf16[2048,40]{0,1:T(8,128)(2,1)}), bf16[2048,1280]{0,1:T(8,128)(2,1)}) %all-gather.6.cloned.1.call-update) | async-done | bytes 5242896 | tf_op jit(solution)/shard_map/all_gather | solution.py:24
  224.6 10.4 %multiply_reduce_fusion = (f32[2048]{0:T(1024)S(1)}, f32[2048,1280]{0,1:T(8,128)S(1)}) fusion(bf16[2048,1280]{0,1:T(8,128)(2,1)} %all-gather.6.cloned.1.call-done, bf16[1280,1280]{1,0:T(8,128)(2,1)} %all-gather.8.cloned.1.call-done), kind=kOutput, calls=%fused_computation.1 | convolution fusion | flops 6716127232 | bytes 19013632 | tf_op jit(solution)/shard_map/dot_general | solution.py:25
  235.0 0.0 copy-done
  235.0 4.7 %fusion.7 = (f32[2048]{0:T(1024)S(1)}, f32[512]{0:T(512)S(1)}, f32[512,2048]{1,0:T(8,128)}) fusion(f32[2048,1280]{0,1:T(8,128)S(1)} %get-tuple-element.9, f32[2048]{0:T(1024)S(1)} %add_rsqrt_fusion, f32[512,1280]{1,0:T(8,128)S(1)} %copy-done, f32[512]{0:T(512)S(1)} %add_rsqrt_fusion.1, f32[]{:T(128)} %bitcast.16), kind=kOutput, calls=%fused_computation.19 | convolution fusion | flops 2697328128 | bytes 17321988 | tf_op jit(solution)/shard_map/dot_general | solution.py:26
  239.7 72.6 %pmax.15 = f32[1,2048]{1,0:T(1,128)S(1)} all-reduce(f32[1,2048]{1,0:T(1,128)S(1)} %bitcast.24), channel_id=1, replica_groups=mesh['img'=32,'txt'=8] {'img'}, use_global_device_ids=true, to_apply=%region_7.0 | all-reduce | flops 2048 | bytes 16384 | tf_op jit(solution)/shard_map/pmax | solution.py:33
  312.3 12.4 %pmax.14 = f32[512,1]{0,1:T(1,128)S(1)} all-reduce(f32[512,1]{0,1:T(1,128)S(1)} %bitcast.25), channel_id=1, replica_groups=mesh['img'=32,'txt'=8] {'txt'}, use_global_device_ids=true, to_apply=%region_3.0 | all-reduce | flops 512 | bytes 4096 | tf_op jit(solution)/shard_map/pmax | solution.py:32
  324.7 3.4 exponential_reduce_fusion
  328.1 12.4 %psum.14 = f32[512,1]{0,1:T(1,128)S(1)} all-reduce(f32[512,1]{0,1:T(1,128)S(1)} %bitcast.22), channel_id=1, replica_groups=mesh['img'=32,'txt'=8] {'txt'}, use_global_device_ids=true, to_apply=%region_5.0 | all-reduce | flops 512 | bytes 4096 | tf_op jit(solution)/shard_map/psum | solution.py:34
  340.6 72.9 %psum.15 = f32[1,2048]{1,0:T(1,128)S(1)} all-reduce(f32[1,2048]{1,0:T(1,128)S(1)} %bitcast.20), channel_id=1, replica_groups=mesh['img'=32,'txt'=8] {'img'}, use_global_device_ids=true, to_apply=%region_9.0 | all-reduce | flops 2048 | bytes 16384 | tf_op jit(solution)/shard_map/psum | solution.py:35
  413.6 6.1 %broadcast_subtract_fusion = (f32[512,2048]{1,0:T(8,128)}, f32[512,2048]{1,0:T(8,128)}) fusion(f32[512,2048]{1,0:T(8,128)} %get-tuple-element.12, f32[2048]{0:T(1024)S(1)} %bitcast.19, f32[512]{0:T(512)S(1)} %bitcast.23), kind=kLoop, calls=%fused_computation.10 | loop fusion | flops 2097152 | bytes 12593152 | tf_op jit(solution)/shard_map/sub | solution.py:37
  (4 shorter events, 0.0 us)
Async XLA Ops:
  7.2 50.4 %all-gather.4.cloned.1.call-start = ((), (), s32[]{:S(2)}) async-start(), calls=%async_computation.1 | async-start | bytes 4792320 | tf_op jit(solution)/shard_map/all_gather | solution.py:21
  7.9 132.5 %all-gather.8.cloned.1.call-start = ((), (), s32[]{:S(2)}) async-start(), calls=%async_computation.3 | async-start | bytes 3379200 | tf_op jit(solution)/shard_map/all_gather | solution.py:23
  8.6 215.9 %all-gather.6.cloned.1.call-start = ((), (), s32[]{:S(2)}) async-start(), calls=%async_computation.2 | async-start | bytes 5406720 | tf_op jit(solution)/shard_map/all_gather | solution.py:24
  11.6 37.6 %all-to-all-start = ((bf16[8,512,208]{1,2,0:T(8,128)(2,1)}), bf16[8,512,208]{1,2,0:T(8,128)(2,1)S(1)}, u32[]{:S(2)}, u32[]{:S(2)}) async-start(bf16[8,512,208]{1,2,0:T(8,128)(2,1)} %stack.2), calls=%async_computation | async-start | bytes 3407872 | tf_op jit(solution)/shard_map/all_to_all | solution.py:19
  63.9 171.1 %copy-start = (f32[512,1280]{1,0:T(8,128)S(1)}, f32[512,1280]{1,0:T(8,128)}, u32[]{:S(2)}) copy-start(f32[512,1280]{1,0:T(8,128)} %get-tuple-element.11) | copy-start | bytes 7864324
Sparse Core Ops, SparseCore 0:
  9.8 47.7 all-gather.3
  60.2 80.1 all-gather.7
  143.0 81.5 all-gather.5
